TPU v7x, 32 devices: a whole 2x2x4 slice. The times are simulated.
32 devices in a mesh: rep: 2 (over y), ep: 16 (over z, x, core).
Axes of the slice: x: 2, y: 2, z: 4, core: 2. Of those that a mesh axis runs over, the one named last changes fastest.
Arguments:
- tokens: bfloat16 [4096, 2048], P(('rep', 'ep')), may hold values from -6 to 6
- expert_ids: int32 [4096, 6], P(('rep', 'ep')), may hold values from 0 to 15, all different within a row; in each aligned block of 128 rows (0 to 127, 128 to 255, ...) at most 64 rows name the same one
- gate_weights: float32 [4096, 6], P(('rep', 'ep')), may hold values from 0.03 to 0.5
- cotangent: bfloat16 [4096, 2048], P(('rep', 'ep')), may hold values from -4 to 4
- w_gate: bfloat16 [16, 2048, 704], P('ep'), may hold values from -0.125 to 0.125
- w_up: bfloat16 [16, 2048, 704], P('ep'), may hold values from -0.125 to 0.125
- w_down: bfloat16 [16, 704, 2048], P('ep'), may hold values from -0.21875 to 0.21875
Outputs:
- mixed: bfloat16 [4096, 2048], P(('rep', 'ep'))
- token_grad: bfloat16 [4096, 2048], P(('rep', 'ep'))
- gate_grad: float32 [4096, 6], P(('rep', 'ep'))
- grad_w_gate: float32 [16, 2048, 704], P('ep', 'rep')
- grad_w_up: float32 [16, 2048, 704], P('ep', 'rep')
- grad_w_down: float32 [16, 704, 2048], P('ep', 'rep')
Inputs may be any that keep to these rules, and one draw needn't show every extreme that they name: `expert_ids`: A token's 6 expert ids are distinct; among the tokens of one device no expert is named by more than 64 choices.
All inputs are finite; a program needn't handle non-finite values.
Results may differ from a plain program's by a relative error of at most 0.0085.
Values may be sent and summed in bfloat16 or wider, within the bound.
A program may use at most 128 MiB of HBM per device.

v0:
```python
import jax
import jax.numpy as jnp
from jax import lax
from jax.sharding import PartitionSpec as P


def hidden_parts(received, gate_matrix, up_matrix):
    gate_pre = jnp.einsum("scd,df->scf", received, gate_matrix, preferred_element_type=jnp.float32)
    up_pre = jnp.einsum("scd,df->scf", received, up_matrix, preferred_element_type=jnp.float32)
    act = (gate_pre * jax.nn.sigmoid(gate_pre) * up_pre).astype(jnp.bfloat16)
    return (gate_pre, up_pre, act)


def project_out(act, down_matrix):
    return jnp.einsum("scf,fd->scd", act, down_matrix, preferred_element_type=jnp.float32).astype(
        jnp.bfloat16
    )


def backward_rows(d_rows, gate_pre, up_pre, gate_matrix, up_matrix, down_matrix):
    act_grad = jnp.einsum("scd,fd->scf", d_rows, down_matrix, preferred_element_type=jnp.float32)
    sigmoid_val = jax.nn.sigmoid(gate_pre)
    silu_val = gate_pre * sigmoid_val
    gate_pre_grad = (
        act_grad * up_pre * sigmoid_val * (1.0 + gate_pre * (1.0 - sigmoid_val))
    ).astype(jnp.bfloat16)
    up_pre_grad = (act_grad * silu_val).astype(jnp.bfloat16)
    row_grad = jnp.einsum(
        "scf,df->scd", gate_pre_grad, gate_matrix, preferred_element_type=jnp.float32
    ) + jnp.einsum("scf,df->scd", up_pre_grad, up_matrix, preferred_element_type=jnp.float32)
    return (gate_pre_grad, up_pre_grad, row_grad.astype(jnp.bfloat16))


def column_product(left_side, right_side):
    return lax.dot_general(
        left_side, right_side, (((0,), (0,)), ((), ())), preferred_element_type=jnp.float32
    )


def per_device(tokens, expert_ids, gate_weights, cotangent, w_gate, w_up, w_down):
    tok_rows, row_width = tokens.shape
    top_count = expert_ids.shape[1]
    expert_count = lax.axis_size("ep")
    capacity = top_count * tok_rows * 4 // (3 * expert_count)
    pair_count = tok_rows * top_count
    gate_matrix = w_gate[0]
    up_matrix = w_up[0]
    down_matrix = w_down[0]
    hidden_width = gate_matrix.shape[1]
    flat_ids = expert_ids.reshape(-1)
    onehot = (flat_ids[:, None] == jnp.arange(expert_count, dtype=jnp.int32)[None, :]).astype(
        jnp.int32
    )
    before = jnp.cumsum(onehot, axis=0) - onehot
    slots = jnp.sum(before * onehot, axis=1)
    slot_index = flat_ids * capacity + slots
    slot_owner = jnp.full((expert_count * capacity,), pair_count, jnp.int32)
    slot_owner = slot_owner.at[slot_index].set(jnp.arange(pair_count, dtype=jnp.int32))
    padded_tokens = jnp.concatenate([tokens, jnp.zeros((1, row_width), tokens.dtype)], axis=0)
    send_rows = padded_tokens[slot_owner // top_count].reshape(expert_count, capacity, row_width)
    scaled = (gate_weights[:, :, None] * cotangent[:, None, :].astype(jnp.float32)).astype(
        jnp.bfloat16
    )
    scaled = jnp.concatenate(
        [scaled.reshape(pair_count, row_width), jnp.zeros((1, row_width), scaled.dtype)], axis=0
    )
    send_cot = scaled[slot_owner].reshape(expert_count, capacity, row_width)
    received = lax.all_to_all(send_rows, "ep", split_axis=0, concat_axis=0, tiled=True)
    gate_pre, up_pre, act = hidden_parts(received, gate_matrix, up_matrix)
    expert_out = project_out(act, down_matrix)
    out_back = lax.all_to_all(expert_out, "ep", split_axis=0, concat_axis=0, tiled=True)
    out_back, received, gate_pre, up_pre, act = (out_back, received, gate_pre, up_pre, act)
    d_rows = lax.all_to_all(send_cot, "ep", split_axis=0, concat_axis=0, tiled=True)
    gate_pre_grad, up_pre_grad, row_grad = backward_rows(
        d_rows, gate_pre, up_pre, gate_matrix, up_matrix, down_matrix
    )
    grad_back = lax.all_to_all(row_grad, "ep", split_axis=0, concat_axis=0, tiled=True)
    picked = (
        out_back.reshape(-1, row_width)[slot_index]
        .reshape(tok_rows, top_count, row_width)
        .astype(jnp.float32)
    )
    mixed = jnp.sum(gate_weights[:, :, None] * picked, axis=1).astype(jnp.bfloat16)
    gate_grad = jnp.sum(cotangent[:, None, :].astype(jnp.float32) * picked, axis=2)
    back_rows = grad_back.reshape(-1, row_width)[slot_index].reshape(tok_rows, top_count, row_width)
    token_grad = jnp.sum(back_rows.astype(jnp.float32), axis=1).astype(jnp.bfloat16)
    flat_rows = received.reshape(-1, row_width)
    flat_drows = d_rows.reshape(-1, row_width)
    flat_act = act.reshape(-1, hidden_width)
    flat_gate_grad = gate_pre_grad.reshape(-1, hidden_width)
    flat_up_grad = up_pre_grad.reshape(-1, hidden_width)
    full_gate = column_product(flat_rows, flat_gate_grad)[None]
    full_up = column_product(flat_rows, flat_up_grad)[None]
    full_down = column_product(flat_act, flat_drows)[None]
    grad_gate, grad_up, grad_down = (
        lax.psum_scatter(
            full_gate.astype(jnp.bfloat16), "rep", scatter_dimension=1, tiled=True
        ).astype(jnp.float32),
        lax.psum_scatter(
            full_up.astype(jnp.bfloat16), "rep", scatter_dimension=1, tiled=True
        ).astype(jnp.float32),
        lax.psum_scatter(
            full_down.astype(jnp.bfloat16), "rep", scatter_dimension=1, tiled=True
        ).astype(jnp.float32),
    )
    return (mixed, token_grad, gate_grad, grad_gate, grad_up, grad_down)


def solution(mesh):
    placed = (
        P(("rep", "ep"), None),
        P(("rep", "ep"), None),
        P(("rep", "ep"), None),
        P(("rep", "ep"), None),
        P("ep", None, None),
        P("ep", None, None),
        P("ep", None, None),
    )
    return jax.shard_map(
        per_device,
        mesh=mesh,
        in_specs=placed,
        out_specs=(
            P(("rep", "ep"), None),
            P(("rep", "ep"), None),
            P(("rep", "ep"), None),
            P("ep", "rep", None),
            P("ep", "rep", None),
            P("ep", "rep", None),
        ),
        check_vma=False,
    )
```

profile of v0, /device:TPU:9, one launch (start us, length us, event | category | flops | bytes accessed | tf_op | source)
XLA Modules:
  0.0 471.9 jit_solution(8298476493254000438)
XLA Ops:
  7.2 0.0 copy-start
  7.2 0.9 copy.22
  8.1 0.1 eq.29
  8.3 0.1 eq.25
  8.4 0.7 broadcast_multiply_fusion
  9.1 1.7 reduce-window.6
  10.8 0.3 slice_reduce_fusion
  11.1 0.1 copy.21
  11.2 0.1 mul.80
  11.4 0.1 fusion.16
  11.5 3.4 scatter_custom_fusion
  14.9 1.1 concatenate.6
  16.0 6.0 %gather_fusion = bf16[1024,2048]{1,0:T(8,128)(2,1)} fusion(bf16[129,2048]{1,0:T(8,128)(2,1)S(1)} %concatenate.6, s32[1024]{0:T(1024)S(1)} %get-tuple-element.18), kind=kCustom, calls=%fused_computation | custom fusion | bytes 8392704 | tf_op jit(solution)/shard_map/gather | solution.py:60
  22.0 6.7 %all-to-all-start = ((bf16[16,64,2048]{2,1,0:T(8,128)(2,1)}), bf16[16,64,2048]{2,1,0:T(8,128)(2,1)}, u32[]{:S(2)}, u32[]{:S(2)}) async-start(bf16[16,64,2048]{2,1,0:T(8,128)(2,1)} %bitcast.74), calls=%async_computation | async-start | bytes 8388608 | tf_op jit(solution)/shard_map/all_to_all | solution.py:68
  28.7 0.0 copy-done.2
  28.7 0.1 copy.20
  28.9 0.1 mul.85
  29.0 0.0 copy-done.1
  29.0 4.3 mul.87
  33.3 8.2 %mul.88 = f32[768,2048]{1,0:T(8,128)} reshape(f32[128,6,2048]{2,1,0:T(8,128)} %mul.87) | data formatting | bytes 12582912 | tf_op jit(solution)/shard_map/mul | solution.py:61
  41.5 3.2 multiply_convert_fusion
  44.7 2.1 concatenate.7
  46.9 11.1 %gather_fusion.2 = bf16[1024,2048]{1,0:T(8,128)(2,1)} fusion(bf16[769,2048]{1,0:T(8,128)(2,1)} %concatenate.7, s32[1024]{0:T(1024)S(1)} %get-tuple-element.17), kind=kCustom, calls=%fused_computation.2 | custom fusion | bytes 8392704 | tf_op jit(solution)/shard_map/gather | solution.py:67
  58.0 61.1 %all-to-all-done = bf16[16,64,2048]{2,1,0:T(8,128)(2,1)} async-done(((bf16[16,64,2048]{2,1,0:T(8,128)(2,1)}), bf16[16,64,2048]{2,1,0:T(8,128)(2,1)}, u32[]{:S(2)}, u32[]{:S(2)}) %all-to-all-start) | async-done | bytes 4194336 | tf_op jit(solution)/shard_map/all_to_all | solution.py:68
  119.1 7.1 %all-to-all-start.2 = ((bf16[16,64,2048]{2,1,0:T(8,128)(2,1)}), bf16[16,64,2048]{2,1,0:T(8,128)(2,1)}, u32[]{:S(2)}, u32[]{:S(2)}) async-start(bf16[16,64,2048]{2,1,0:T(8,128)(2,1)} %bitcast.75), calls=%async_computation.2 | async-start | bytes 8388608 | tf_op jit(solution)/shard_map/all_to_all | solution.py:73
  126.1 0.2 reduce-scatter.4.cloned.1.call-start
  126.3 0.0 copy-start.3
  126.3 8.3 %fusion.12 = f32[16,64,704]{2,1,0:T(8,128)} fusion(bf16[16,64,2048]{2,1,0:T(8,128)(2,1)} %all-to-all-done, bf16[1,2048,704]{1,2,0:T(8,128)(2,1)} %param.11), kind=kOutput, calls=%fused_computation.29 | convolution fusion | flops 2952790016 | bytes 9961472 | tf_op jit(solution)/shard_map/scd,df->scf/dot_general | solution.py:8
  134.7 0.0 copy-done.3
  134.7 7.3 %fusion.8 = f32[16,64,704]{2,1,0:T(8,128)} fusion(bf16[16,64,2048]{2,1,0:T(8,128)(2,1)} %all-to-all-done, bf16[1,2048,704]{1,2,0:T(8,128)(2,1)S(1)} %copy-done.3), kind=kOutput, calls=%fused_computation.25 | convolution fusion | flops 2952790016 | bytes 9961472 | tf_op jit(solution)/shard_map/scd,df->scf/dot_general | solution.py:9
  142.0 74.5 %all-to-all-done.2 = bf16[16,64,2048]{2,1,0:T(8,128)(2,1)} async-done(((bf16[16,64,2048]{2,1,0:T(8,128)(2,1)}), bf16[16,64,2048]{2,1,0:T(8,128)(2,1)}, u32[]{:S(2)}, u32[]{:S(2)}) %all-to-all-start.2) | async-done | bytes 4194336 | tf_op jit(solution)/shard_map/all_to_all | solution.py:73
  216.4 0.0 copy-done
  216.4 10.1 %multiply_convert_fusion.1 = (bf16[16,64,704]{2,1,0:T(8,128)(2,1)}, bf16[16,64,704]{2,1,0:T(8,128)(2,1)S(1)}, bf16[16,64,704]{2,1,0:T(8,128)(2,1)}) fusion(f32[16,64,704]{2,1,0:T(8,128)} %fusion.12, f32[16,64,704]{2,1,0:T(8,128)} %fusion.8, bf16[16,64,2048]{2,1,0:T(8,128)(2,1)} %all-to-all-done.2, bf16[1,704,2048]{2,1,0:T(8,128)(2,1)S(1)} %copy-done), kind=kOutput, calls=%fused_computation.13 | convolution fusion | flops 2963603456 | bytes 17170432 | tf_op jit(solution)/shard_map/scd,fd->scf/dot_general | solution.py:21
  226.6 1.1 copy-done.6
  227.7 7.2 %fusion.1 = bf16[1,2048,704]{1,2,0:T(8,128)(2,1)} fusion(bf16[16,64,2048]{2,1,0:T(8,128)(2,1)} %all-to-all-done, bf16[16,64,704]{2,1,0:T(8,128)(2,1)S(1)} %get-tuple-element.15), kind=kOutput, calls=%fused_computation.18 | convolution fusion | flops 2954231808 | bytes 8519680 | tf_op jit(solution)/shard_map/dot_general | solution.py:35
  234.9 0.0 reduce-scatter.4.cloned.1.call-update
  235.0 0.0 copy-start.4
  235.0 0.0 copy-start.5
  235.0 5.9 %fusion.10 = f32[16,64,2048]{2,1,0:T(8,128)S(1)} fusion(bf16[16,64,704]{2,1,0:T(8,128)(2,1)} %copy-done.6, bf16[1,2048,704]{1,2,0:T(8,128)(2,1)} %param.11), kind=kOutput, calls=%fused_computation.27 | convolution fusion | flops 2952790016 | bytes 12713984 | tf_op jit(solution)/shard_map/scf,df->scd/dot_general | solution.py:28
  240.8 0.0 copy-done.4
  240.9 5.0 %add_convert_fusion = bf16[16,64,2048]{2,1,0:T(8,128)(2,1)} fusion(f32[16,64,2048]{2,1,0:T(8,128)S(1)} %fusion.10, bf16[16,64,704]{2,1,0:T(8,128)(2,1)S(1)} %copy-done.5, bf16[1,2048,704]{1,2,0:T(8,128)(2,1)S(1)} %copy-done.4), kind=kOutput, calls=%fused_computation.6 | convolution fusion | flops 2956984320 | bytes 16908288 | tf_op jit(solution)/shard_map/scf,df->scd/dot_general | solution.py:30
  245.9 7.1 %all-to-all-start.3 = ((bf16[16,64,2048]{2,1,0:T(8,128)(2,1)}), bf16[16,64,2048]{2,1,0:T(8,128)(2,1)}, u32[]{:S(2)}, u32[]{:S(2)}) async-start(bf16[16,64,2048]{2,1,0:T(8,128)(2,1)} %add_convert_fusion), calls=%async_computation.3 | async-start | bytes 8388608 | tf_op jit(solution)/shard_map/all_to_all | solution.py:77
  252.9 0.0 reduce-scatter.6.cloned.1.call-start
  253.0 7.6 %fusion.2 = bf16[1,2048,704]{1,2,0:T(8,128)(2,1)} fusion(bf16[16,64,2048]{2,1,0:T(8,128)(2,1)} %all-to-all-done, bf16[16,64,704]{2,1,0:T(8,128)(2,1)} %get-tuple-element.14), kind=kOutput, calls=%fused_computation.19 | convolution fusion | flops 2954231808 | bytes 8519680 | tf_op jit(solution)/shard_map/dot_general | solution.py:35
  260.6 0.0 reduce-scatter.6.cloned.1.call-update
  260.6 6.5 %convolution_convert_fusion = bf16[16,64,2048]{2,1,0:T(8,128)(2,1)} fusion(bf16[16,64,704]{2,1,0:T(8,128)(2,1)} %get-tuple-element.16, bf16[1,704,2048]{2,1,0:T(8,128)(2,1)S(1)} %copy-done), kind=kOutput, calls=%fused_computation.12 | convolution fusion | flops 2954887168 | bytes 8519680 | tf_op jit(solution)/shard_map/scf,fd->scd/dot_general | solution.py:15
  267.0 76.2 %all-to-all-done.3 = bf16[16,64,2048]{2,1,0:T(8,128)(2,1)} async-done(((bf16[16,64,2048]{2,1,0:T(8,128)(2,1)}), bf16[16,64,2048]{2,1,0:T(8,128)(2,1)}, u32[]{:S(2)}, u32[]{:S(2)}) %all-to-all-start.3) | async-done | bytes 4194336 | tf_op jit(solution)/shard_map/all_to_all | solution.py:77
  343.3 7.1 %all-to-all-start.1 = ((bf16[16,64,2048]{2,1,0:T(8,128)(2,1)}), bf16[16,64,2048]{2,1,0:T(8,128)(2,1)}, u32[]{:S(2)}, u32[]{:S(2)}) async-start(bf16[16,64,2048]{2,1,0:T(8,128)(2,1)} %convolution_convert_fusion), calls=%async_computation.1 | async-start | bytes 8388608 | tf_op jit(solution)/shard_map/all_to_all | solution.py:71
  350.3 0.0 reduce-scatter.8.cloned.1.call-start
  350.4 7.5 %fusion.3 = bf16[1,704,2048]{2,1,0:T(8,128)(2,1)} fusion(bf16[16,64,704]{2,1,0:T(8,128)(2,1)} %get-tuple-element.16, bf16[16,64,2048]{2,1,0:T(8,128)(2,1)} %all-to-all-done.2), kind=kOutput, calls=%fused_computation.20 | convolution fusion | flops 2954231808 | bytes 8519680 | tf_op jit(solution)/shard_map/dot_general | solution.py:35
  357.8 0.0 reduce-scatter.8.cloned.1.call-update
  357.9 1.2 convert_element_type.80
  359.0 3.3 convert_element_type.87
  362.3 3.5 convert_element_type.90
  365.8 33.3 %reduce-scatter.8.cloned.1.call-done = bf16[1,352,2048]{2,1,0:T(8,128)(2,1)} async-done(((bf16[1,704,2048]{2,1,0:T(8,128)(2,1)}), bf16[1,352,2048]{2,1,0:T(8,128)(2,1)}) %reduce-scatter.8.cloned.1.call-update) | async-done | bytes 1441808 | tf_op jit(solution)/shard_map/reduce_scatter | solution.py:102
  399.1 3.3 convert_element_type.93
  402.4 10.1 %gather_fusion.3 = bf16[768,2048]{1,0:T(8,128)(2,1)} fusion(bf16[1024,2048]{1,0:T(8,128)(2,1)} %bitcast.10, s32[1024]{0:T(1024)S(1)} %pad_clamp_fusion), kind=kCustom, calls=%fused_computation.3 | custom fusion | bytes 6294528 | tf_op jit(solution)/shard_map/gather | solution.py:85
  412.4 6.3 %reshape.105 = bf16[128,6,2048]{2,1,0:T(8,128)(2,1)} reshape(bf16[768,2048]{1,0:T(8,128)(2,1)} %gather_fusion.3) | data formatting | bytes 6291456 | tf_op jit(solution)/shard_map/reshape | solution.py:85
  418.7 5.7 %reduce_sum.44 = bf16[128,2048]{1,0:T(8,128)(2,1)} reduce(bf16[128,6,2048]{2,1,0:T(8,128)(2,1)} %reshape.105, bf16[]{:T(256)} %constant.12.clone.1), dimensions={1}, to_apply=%region_5.6 | reduce | flops 1310720 | bytes 3670018 | tf_op jit(solution)/shard_map/reduce_sum | solution.py:86
  424.4 16.3 %all-to-all-done.1 = bf16[16,64,2048]{2,1,0:T(8,128)(2,1)} async-done(((bf16[16,64,2048]{2,1,0:T(8,128)(2,1)}), bf16[16,64,2048]{2,1,0:T(8,128)(2,1)}, u32[]{:S(2)}, u32[]{:S(2)}) %all-to-all-start.1) | async-done | bytes 4194336 | tf_op jit(solution)/shard_map/all_to_all | solution.py:71
  440.6 9.8 %gather_fusion.1 = bf16[768,2048]{1,0:T(8,128)(2,1)} fusion(bf16[1024,2048]{1,0:T(8,128)(2,1)} %bitcast.8, s32[1024]{0:T(1024)S(1)} %pad_clamp_fusion), kind=kCustom, calls=%fused_computation.1 | custom fusion | bytes 6294528 | tf_op jit(solution)/shard_map/gather | solution.py:79
  450.4 6.6 %reshape.106 = f32[128,6,2048]{2,1,0:T(8,128)} reshape(bf16[768,2048]{1,0:T(8,128)(2,1)} %gather_fusion.1) | data formatting | bytes 9437184 | tf_op jit(solution)/shard_map/convert_element_type | solution.py:81
  457.0 7.3 %multiply_reduce_fusion = (f32[128,6]{1,0:T(8,128)S(1)}, bf16[128,2048]{1,0:T(8,128)(2,1)}) fusion(f32[128,6,2048]{2,1,0:T(8,128)} %reshape.106, f32[128,2048]{1,0:T(8,128)} %convert_element_type.80, f32[128,6]{1,0:T(8,128)S(1)} %copy.20), kind=kLoop, calls=%fused_computation.5 | loop fusion | flops 6028544 | bytes 7870464 | tf_op jit(solution)/shard_map/reduce_sum | solution.py:84
  464.3 0.7 copy.26
  (12 shorter events, 0.1 us)
Async XLA Ops:
  7.2 209.3 %copy-start = (bf16[1,704,2048]{2,1,0:T(8,128)(2,1)S(1)}, bf16[1,704,2048]{2,1,0:T(8,128)(2,1)}, u32[]{:S(2)}) copy-start(bf16[1,704,2048]{2,1,0:T(8,128)(2,1)} %param.13) | copy-start | bytes 8650756
  22.0 6.7 %copy-start.2 = (f32[128,6]{0,1:T(8,128)S(1)}, f32[128,6]{0,1:T(8,128)}, u32[]{:S(2)}) copy-start(f32[128,6]{0,1:T(8,128)} %param.9) | copy-start | bytes 9220
  22.0 7.0 %copy-start.1 = (bf16[128,2048]{1,0:T(8,128)(2,1)S(1)}, bf16[128,2048]{1,0:T(8,128)(2,1)}, u32[]{:S(2)}) copy-start(bf16[128,2048]{1,0:T(8,128)(2,1)} %param.10) | copy-start | bytes 1572868
  22.0 97.0 %all-to-all-start = ((bf16[16,64,2048]{2,1,0:T(8,128)(2,1)}), bf16[16,64,2048]{2,1,0:T(8,128)(2,1)}, u32[]{:S(2)}, u32[]{:S(2)}) async-start(bf16[16,64,2048]{2,1,0:T(8,128)(2,1)} %bitcast.74), calls=%async_computation | async-start | bytes 8388608 | tf_op jit(solution)/shard_map/all_to_all | solution.py:68
  119.1 97.4 %all-to-all-start.2 = ((bf16[16,64,2048]{2,1,0:T(8,128)(2,1)}), bf16[16,64,2048]{2,1,0:T(8,128)(2,1)}, u32[]{:S(2)}, u32[]{:S(2)}) async-start(bf16[16,64,2048]{2,1,0:T(8,128)(2,1)} %bitcast.75), calls=%async_computation.2 | async-start | bytes 8388608 | tf_op jit(solution)/shard_map/all_to_all | solution.py:73
  126.1 232.9 %reduce-scatter.4.cloned.1.call-start = ((), (), s32[]{:S(2)}) async-start(), calls=%async_computation.7 | async-start | bytes 4325376 | tf_op jit(solution)/shard_map/reduce_scatter | solution.py:96
  126.3 8.4 %copy-start.3 = (bf16[1,2048,704]{1,2,0:T(8,128)(2,1)S(1)}, bf16[1,2048,704]{1,2,0:T(8,128)(2,1)}, u32[]{:S(2)}) copy-start(bf16[1,2048,704]{1,2,0:T(8,128)(2,1)} %param.12) | copy-start | bytes 8650756
  226.6 1.1 copy-start.6
  235.0 5.9 %copy-start.4 = (bf16[1,2048,704]{1,2,0:T(8,128)(2,1)S(1)}, bf16[1,2048,704]{1,2,0:T(8,128)(2,1)}, u32[]{:S(2)}) copy-start(bf16[1,2048,704]{1,2,0:T(8,128)(2,1)} %param.12) | copy-start | bytes 8650756
  235.0 5.9 %copy-start.5 = (bf16[16,64,704]{2,1,0:T(8,128)(2,1)S(1)}, bf16[16,64,704]{2,1,0:T(8,128)(2,1)}, u32[]{:S(2)}) copy-start(bf16[16,64,704]{2,1,0:T(8,128)(2,1)} %get-tuple-element.14) | copy-start | bytes 4325380
  245.9 97.4 %all-to-all-start.3 = ((bf16[16,64,2048]{2,1,0:T(8,128)(2,1)}), bf16[16,64,2048]{2,1,0:T(8,128)(2,1)}, u32[]{:S(2)}, u32[]{:S(2)}) async-start(bf16[16,64,2048]{2,1,0:T(8,128)(2,1)} %add_convert_fusion), calls=%async_computation.3 | async-start | bytes 8388608 | tf_op jit(solution)/shard_map/all_to_all | solution.py:77
  252.9 109.4 %reduce-scatter.6.cloned.1.call-start = ((), (), s32[]{:S(2)}) async-start(), calls=%async_computation.8 | async-start | bytes 4325376 | tf_op jit(solution)/shard_map/reduce_scatter | solution.py:99
  343.3 97.4 %all-to-all-start.1 = ((bf16[16,64,2048]{2,1,0:T(8,128)(2,1)}), bf16[16,64,2048]{2,1,0:T(8,128)(2,1)}, u32[]{:S(2)}, u32[]{:S(2)}) async-start(bf16[16,64,2048]{2,1,0:T(8,128)(2,1)} %convolution_convert_fusion), calls=%async_computation.1 | async-start | bytes 8388608 | tf_op jit(solution)/shard_map/all_to_all | solution.py:71
  350.3 48.8 %reduce-scatter.8.cloned.1.call-start = ((), (), s32[]{:S(2)}) async-start(), calls=%async_computation.9 | async-start | bytes 4325376 | tf_op jit(solution)/shard_map/reduce_scatter | solution.py:102
Sparse Core Ops, SparseCore 0:
  235.1 42.0 reduce-scatter.3
  280.1 40.4 reduce-scatter.5
  358.0 41.0 reduce-scatter.7
where the time goes:
time: 480 us; the launch traced here: 472 us
  waiting for transfers between devices  261 us (54%)
  local copies, waits for them, and re-layouts  72.8 us (15%)
  matrix products  65.3 us (14%)
  other arithmetic  29.9 us (6%)
  starting transfers between devices  28.2 us (6%)
  between operations  14.4 us (3%)
    all_to_all x1, waiting for transfers between devices, per_device(): lax.all_to_all(row_grad, 'ep', split_axis=0, concat_axis=0, tiled=True)  76.2 us
    all_to_all x1, waiting for transfers between devices, per_device(): lax.all_to_all(send_cot, 'ep', split_axis=0, concat_axis=0, tiled=True)  74.5 us
    all_to_all x1, waiting for transfers between devices, per_device(): lax.all_to_all(send_rows, 'ep', split_axis=0, concat_axis=0, tiled=True)  61.1 us
    reduce_scatter x1, waiting for transfers between devices, per_device(): lax.psum_scatter(full_down.astype(jnp.bfloat16), 'rep', scatter_dimension...  33.3 us
    dot_general x3, matrix products, column_product(): lax.dot_general(left_side, right_side, (((0,), (0,)), ((), ())), preferre...  22.3 us
    all_to_all x1, waiting for transfers between devices, per_device(): lax.all_to_all(expert_out, 'ep', split_axis=0, concat_axis=0, tiled=True)  16.3 us
    mul x2, local copies, waits for them, and re-layouts, per_device(): gate_weights[:, :, None] * cotangent[:, None, :].astype(jnp.float32)  12.5 us
    gather x1, local copies, waits for them, and re-layouts, per_device(): send_cot = scaled[slot_owner].reshape(expert_count, capacity, row_width)  11.1 us
  transfers between devices with their start and end apart: 7, of which 5 were waited for; matrix products, arithmetic and copies ran while one was open for 23% of the time, Pallas kernels for 0%

commit v1 on v0

v1 whole, which is shorter than its diff:
```python
import jax
import jax.numpy as jnp
from jax import lax
from jax.sharding import PartitionSpec as P


def matmul(left, right, left_dim, right_dim):
    return lax.dot_general(
        left, right, (((left_dim,), (right_dim,)), ((), ())), preferred_element_type=jnp.float32
    )


def per_device(tokens, expert_ids, gate_weights, cotangent, w_gate, w_up, w_down):
    tok_rows, row_width = tokens.shape
    top_count = expert_ids.shape[1]
    expert_count = lax.axis_size("ep")
    capacity = top_count * tok_rows * 4 // (3 * expert_count)
    rows = expert_count * capacity
    gate_matrix = w_gate[0]
    up_matrix = w_up[0]
    down_matrix = w_down[0]

    chosen = expert_ids[:, :, None] == jnp.arange(expert_count, dtype=jnp.int32)[None, None, :]
    weights = jnp.sum(jnp.where(chosen, gate_weights[:, :, None], 0.0), axis=1)
    mine = lax.all_to_all(weights.T, "ep", split_axis=0, concat_axis=0, tiled=True)

    all_tokens = lax.all_gather(tokens, "ep", axis=0, tiled=True)
    all_cot = lax.all_gather(cotangent, "ep", axis=0, tiled=True)

    named = mine > 0.0
    before = jnp.cumsum(named.astype(jnp.int32), axis=1) - 1
    slot = jnp.where(named, before, -1)
    pick = slot[:, None, :] == jnp.arange(capacity, dtype=jnp.int32)[None, :, None]
    pick_b = pick.astype(jnp.bfloat16)
    gate = jnp.sum(jnp.where(pick, mine[:, None, :], 0.0), axis=2).reshape(rows, 1)

    def dispatch(everything):
        blocks = everything.reshape(expert_count, tok_rows, row_width)
        return (
            jnp.einsum("sct,std->scd", pick_b, blocks, preferred_element_type=jnp.float32)
            .astype(jnp.bfloat16)
            .reshape(rows, row_width)
        )

    def collect(part):
        part = part.astype(jnp.bfloat16).reshape(expert_count, capacity, row_width)
        spread = jnp.einsum("sct,scd->std", pick_b, part, preferred_element_type=jnp.float32)
        return lax.psum_scatter(
            spread.astype(jnp.bfloat16).reshape(expert_count * tok_rows, row_width),
            "ep",
            scatter_dimension=0,
            tiled=True,
        )

    def over_rep(part):
        return lax.psum_scatter(
            part.astype(jnp.bfloat16)[None], "rep", scatter_dimension=1, tiled=True
        ).astype(jnp.float32)

    x_rows = dispatch(all_tokens)
    gate_pre = matmul(x_rows, gate_matrix, 1, 0)
    up_pre = matmul(x_rows, up_matrix, 1, 0)
    sigmoid_val = jax.nn.sigmoid(gate_pre)
    silu_val = gate_pre * sigmoid_val
    act = silu_val * up_pre
    weighted = (gate * act).astype(jnp.bfloat16)
    mixed = collect(matmul(weighted, down_matrix, 1, 0))

    c_rows = dispatch(all_cot)
    grad_down = over_rep(matmul(weighted, c_rows, 0, 0))
    back = matmul(c_rows, down_matrix, 1, 1)
    act_grad = gate * back
    gate_pre_grad = (
        act_grad * up_pre * sigmoid_val * (1.0 + gate_pre * (1.0 - sigmoid_val))
    ).astype(jnp.bfloat16)
    up_pre_grad = (act_grad * silu_val).astype(jnp.bfloat16)
    pair_grad = jnp.sum(act * back, axis=1).reshape(expert_count, capacity, 1)
    row_grad = matmul(gate_pre_grad, gate_matrix, 1, 1) + matmul(up_pre_grad, up_matrix, 1, 1)
    token_grad = collect(row_grad)
    grad_gate = over_rep(matmul(x_rows, gate_pre_grad, 0, 0))
    grad_up = over_rep(matmul(x_rows, up_pre_grad, 0, 0))

    token_pair = jnp.sum(jnp.where(pick, pair_grad, 0.0), axis=1)
    pairs = lax.all_to_all(token_pair, "ep", split_axis=0, concat_axis=0, tiled=True)
    gate_grad = jnp.sum(jnp.where(chosen, pairs.T[:, None, :], 0.0), axis=2)
    return (mixed, token_grad, gate_grad, grad_gate, grad_up, grad_down)


def solution(mesh):
    placed = (
        P(("rep", "ep"), None),
        P(("rep", "ep"), None),
        P(("rep", "ep"), None),
        P(("rep", "ep"), None),
        P("ep", None, None),
        P("ep", None, None),
        P("ep", None, None),
    )
    return jax.shard_map(
        per_device,
        mesh=mesh,
        in_specs=placed,
        out_specs=(
            P(("rep", "ep"), None),
            P(("rep", "ep"), None),
            P(("rep", "ep"), None),
            P("ep", "rep", None),
            P("ep", "rep", None),
            P("ep", "rep", None),
        ),
        check_vma=False,
    )
```

time: 480 us -> 544 us (1.13); the launches traced: 472 us -> 542 us
  waiting for transfers between devices: 261 us -> 420 us
  local copies, waits for them, and re-layouts: 72.8 us -> 1.45 us
  starting transfers between devices: 28.2 us -> 0.5 us
  blocking collectives: 0 us -> 19.8 us
  other arithmetic: 29.9 us -> 17.8 us
    reduce_scatter x3 -> x5, waiting for transfers between devices: 33.3 us -> 284 us  [the longest x2 216 us: collect(): lax.psum_scatter(spread.astype(jnp.bfloat16).reshape(expert_count * tok_r...]
    all_to_all x4 -> x0, waiting for transfers between devices: 228 us -> none  [the longest x1 76.2 us: per_device(): lax.all_to_all(row_grad, 'ep', split_axis=0, concat_axis=0, tiled=True)]
    all_gather x0 -> x2, waiting for transfers between devices: none -> 134 us  [the longest x1 68.8 us: per_device(): all_tokens = lax.all_gather(tokens, 'ep', axis=0, tiled=True)]
    gather x4 -> x0, local copies, waits for them, and re-layouts: 37 us -> none  [the longest x1 11.1 us: per_device(): send_cot = scaled[slot_owner].reshape(expert_count, capacity, row_width)]
    all_to_all x4 -> x0, starting transfers between devices: 27.9 us -> none  [the longest x1 7.07 us: per_device(): lax.all_to_all(row_grad, 'ep', split_axis=0, concat_axis=0, tiled=True)]
    all_to_all x0 -> x2, blocking collectives: none -> 19.8 us  [the longest x1 11.1 us: per_device(): lax.all_to_all(weights.T, 'ep', split_axis=0, concat_axis=0, tiled=True)]
    mul x5 -> x1, local copies, waits for them, and re-layouts: 12.9 us -> 0.07 us  [per_device(): weighted = (gate * act).astype(jnp.bfloat16)]
    reduce_sum x3, other arithmetic: 13 us -> 1.73 us  [the longest x1 0.72 us: per_device(): weights = jnp.sum(jnp.where(chosen, gate_weights[:, :, None], 0.0), axis=1)]
  transfers between devices with their start and end apart: 7 -> 7, of which waited for: 5 -> 6; matrix products, arithmetic and copies ran while one was open for 23% -> 11% of each run, Pallas kernels for 0% -> 0%
where the time goes in v1:
time: 544 us; the launch traced here: 542 us
  waiting for transfers between devices  420 us (77%)
  matrix products  68 us (12%)
  blocking collectives  19.8 us (4%)
  other arithmetic  17.8 us (3%)
  between operations  14.3 us (3%)
    reduce_scatter x2, waiting for transfers between devices, collect(): lax.psum_scatter(spread.astype(jnp.bfloat16).reshape(expert_count * tok_r...  216 us
    all_gather x1, waiting for transfers between devices, per_device(): all_tokens = lax.all_gather(tokens, 'ep', axis=0, tiled=True)  68.8 us
    reduce_scatter x3, waiting for transfers between devices, over_rep(): lax.psum_scatter(part.astype(jnp.bfloat16)[None], 'rep', scatter_dimensio...  68.3 us
    all_gather x1, waiting for transfers between devices, per_device(): all_cot = lax.all_gather(cotangent, 'ep', axis=0, tiled=True)  65.3 us
    dot_general x9, matrix products, matmul(): lax.dot_general(left, right, (((left_dim,), (right_dim,)), ((), ())), pre...  45.4 us
    dot_general x2, matrix products, dispatch(): jnp.einsum('sct,std->scd', pick_b, blocks, preferred_element_type=jnp.flo...  11.3 us
    dot_general x2, matrix products, collect(): jnp.einsum('sct,scd->std', pick_b, part, preferred_element_type=jnp.float32)  11.2 us
    all_to_all x1, blocking collectives, per_device(): lax.all_to_all(weights.T, 'ep', split_axis=0, concat_axis=0, tiled=True)  11.1 us
  transfers between devices with their start and end apart: 7, of which 6 were waited for; matrix products, arithmetic and copies ran while one was open for 11% of the time, Pallas kernels for 0%

profile of v1, /device:TPU:9, one launch (start us, length us, event | category | flops | bytes accessed | tf_op | source)
XLA Modules:
  0.0 541.8 jit_solution(6783259466718031855)
XLA Ops:
  7.2 0.0 copy-start
  7.2 0.0 all-gather.5.cloned.1.call-start
  7.2 0.7 all-gather.5.cloned.1.call-update
  7.9 0.0 all-gather.3.cloned.1.call-start
  8.0 0.7 all-gather.3.cloned.1.call-update
  8.7 0.0 reduce-scatter.14.cloned.1.call-start
  8.7 0.7 select_reduce_fusion.3
  9.4 11.1 %all_to_all.24 = f32[16,1,128]{2,1,0:T(1,128)S(1)} all-to-all(f32[16,1,128]{2,1,0:T(1,128)S(1)} %bitcast.78), channel_id=1, replica_groups=mesh['rep'=2,'ep'=16] {'ep'}, dimensions={0} | all-to-all | bytes 16384 | tf_op jit(solution)/shard_map/all_to_all | solution.py:25
  20.5 0.3 reduce_window_sum.11
  20.8 65.3 %all-gather.5.cloned.1.call-done = bf16[2048,2048]{1,0:T(8,128)(2,1)} async-done(((bf16[128,2048]{1,0:T(8,128)(2,1)}), bf16[2048,2048]{1,0:T(8,128)(2,1)}) %all-gather.5.cloned.1.call-update) | async-done | bytes 8388624 | tf_op jit(solution)/shard_map/all_gather | solution.py:28
  86.1 6.6 %convolution_convert_fusion.3 = bf16[16,64,2048]{2,1,0:T(8,128)(2,1)} fusion(bf16[16,128,2048]{2,1,0:T(8,128)(2,1)} %bitcast.64, s32[16,128]{1,0:T(8,128)S(1)} %select_bitcast_fusion), kind=kOutput, calls=%fused_computation.4 | convolution fusion | flops 539099136 | bytes 12591104 | tf_op jit(solution)/shard_map/sct,std->scd/dot_general | solution.py:40
  92.7 68.8 %all-gather.3.cloned.1.call-done = bf16[2048,2048]{1,0:T(8,128)(2,1)} async-done(((bf16[128,2048]{1,0:T(8,128)(2,1)}), bf16[2048,2048]{1,0:T(8,128)(2,1)}) %all-gather.3.cloned.1.call-update) | async-done | bytes 8388624 | tf_op jit(solution)/shard_map/all_gather | solution.py:27
  161.4 0.0 copy-start.10
  161.4 4.8 convolution_convert_fusion.4
  166.2 0.0 copy-start.1
  166.2 0.0 copy-done.10
  166.2 0.0 copy-start.9
  166.2 3.2 fusion.7
  169.4 0.0 copy-done.1
  169.4 0.1 copy-done.9
  169.6 3.2 fusion.11
  172.7 0.0 copy-start.5
  172.8 0.0 copy-done.4
  172.8 0.0 copy-done
  172.8 0.0 copy-done.2
  172.8 5.1 multiply_reduce_fusion
  177.9 0.0 copy-done.5
  177.9 0.1 broadcast_in_dim.68
  178.0 0.4 select_reduce_fusion
  178.4 0.1 mul.40
  178.5 5.9 %multiply_convert_fusion = (bf16[1024,704]{0,1:T(8,128)(2,1)}, bf16[1024,704]{0,1:T(8,128)(2,1)}, bf16[1024,704]{0,1:T(8,128)(2,1)S(1)}) fusion(f32[1024,704]{0,1:T(8,128)} %get-tuple-element.14, f32[1024]{0:T(1024)S(1)} %mul.40, f32[1024,704]{0,1:T(8,128)} %copy-done.5, f32[1024,704]{0,1:T(8,128)} %copy-done.4), kind=kLoop, calls=%fused_computation.23 | loop fusion | flops 12255232 | bytes 12980224 | tf_op jit(solution)/shard_map/convert_element_type | solution.py:76
  184.4 1.1 copy-done.7
  185.5 0.0 copy-done.3
  185.5 4.5 fusion
  189.9 0.0 reduce-scatter.14.cloned.1.call-update
  190.0 0.0 reduce-scatter.12.cloned.1.call-start
  190.0 7.4 %fusion.2 = bf16[1,2048,704]{1,2,0:T(8,128)(2,1)} fusion(bf16[1024,704]{0,1:T(8,128)(2,1)} %get-tuple-element.10, bf16[1024,2048]{1,0:T(8,128)(2,1)} %bitcast.68), kind=kOutput, calls=%fused_computation.11 | convolution fusion | flops 2954231808 | bytes 8519680 | tf_op jit(solution)/shard_map/dot_general | solution.py:8
  197.4 0.0 reduce-scatter.12.cloned.1.call-update
  197.4 0.0 reduce-scatter.10.cloned.1.call-start
  197.4 7.4 %fusion.1 = bf16[1,2048,704]{1,2,0:T(8,128)(2,1)} fusion(bf16[1024,704]{0,1:T(8,128)(2,1)} %get-tuple-element.11, bf16[1024,2048]{1,0:T(8,128)(2,1)} %bitcast.69), kind=kOutput, calls=%fused_computation.10 | convolution fusion | flops 2954231808 | bytes 8519680 | tf_op jit(solution)/shard_map/dot_general | solution.py:8
  204.8 0.0 reduce-scatter.10.cloned.1.call-update
  204.8 0.0 reduce-scatter.6.cloned.1.call-start
  204.9 5.1 convolution_convert_fusion.2
  210.0 5.6 %convolution_convert_fusion.1 = bf16[16,128,2048]{2,1,0:T(8,128)(2,1)} fusion(bf16[16,64,2048]{2,1,0:T(8,128)(2,1)S(1)} %bitcast.73, s32[16,128]{1,0:T(8,128)S(1)} %select_bitcast_fusion), kind=kOutput, calls=%fused_computation.2 | convolution fusion | flops 541196288 | bytes 12591104 | tf_op jit(solution)/shard_map/sct,scd->std/dot_general | solution.py:47
  215.6 0.0 reduce-scatter.6.cloned.1.call-update
  215.7 0.3 reduce-scatter.8.cloned.1.call-start
  215.9 0.0 copy-start.6
  215.9 0.0 copy-start.11
  215.9 5.9 %fusion.9 = f32[1024,2048]{1,0:T(8,128)S(1)} fusion(bf16[1024,704]{0,1:T(8,128)(2,1)} %get-tuple-element.11, bf16[1,2048,704]{1,2,0:T(8,128)(2,1)} %param.11), kind=kOutput, calls=%fused_computation.18 | convolution fusion | flops 2952790016 | bytes 12713984 | tf_op jit(solution)/shard_map/dot_general | solution.py:8
  221.8 0.0 copy-done.6
  221.8 0.0 copy-done.11
  221.9 3.8 add_convert_fusion
  225.6 5.6 %convolution_convert_fusion = bf16[16,128,2048]{2,1,0:T(8,128)(2,1)} fusion(bf16[16,64,2048]{2,1,0:T(8,128)(2,1)S(1)} %bitcast.72, s32[16,128]{1,0:T(8,128)S(1)} %select_bitcast_fusion), kind=kOutput, calls=%fused_computation.1 | convolution fusion | flops 541196288 | bytes 12591104 | tf_op jit(solution)/shard_map/sct,scd->std/dot_general | solution.py:47
  231.2 0.0 reduce-scatter.8.cloned.1.call-update
  231.2 8.7 %all_to_all.25 = f32[16,1,128]{2,1,0:T(1,128)S(1)} all-to-all(f32[16,1,128]{2,1,0:T(1,128)S(1)} %bitcast.76), channel_id=1, replica_groups=mesh['rep'=2,'ep'=16] {'ep'}, dimensions={0} | all-to-all | bytes 16384 | tf_op jit(solution)/shard_map/all_to_all | solution.py:84
  240.0 0.0 copy-done.8
  240.0 0.6 select_reduce_fusion.2
  240.6 3.3 convert_element_type.65
  243.9 28.4 %reduce-scatter.12.cloned.1.call-done = bf16[1,1024,704]{1,2,0:T(8,128)(2,1)} async-done(((bf16[1,2048,704]{1,2,0:T(8,128)(2,1)}), bf16[1,1024,704]{1,2,0:T(8,128)(2,1)}) %reduce-scatter.12.cloned.1.call-update) | async-done | bytes 1441808 | tf_op jit(solution)/shard_map/reduce_scatter | solution.py:56
  272.3 3.3 convert_element_type.63
  275.6 39.9 %reduce-scatter.10.cloned.1.call-done = bf16[1,1024,704]{1,2,0:T(8,128)(2,1)} async-done(((bf16[1,2048,704]{1,2,0:T(8,128)(2,1)}), bf16[1,1024,704]{1,2,0:T(8,128)(2,1)}) %reduce-scatter.10.cloned.1.call-update) | async-done | bytes 1441808 | tf_op jit(solution)/shard_map/reduce_scatter | solution.py:56
  315.5 3.3 convert_element_type.61
  318.8 106.5 %reduce-scatter.6.cloned.1.call-done = bf16[128,2048]{1,0:T(8,128)(2,1)} async-done(((bf16[2048,2048]{1,0:T(8,128)(2,1)}), bf16[128,2048]{1,0:T(8,128)(2,1)}) %reduce-scatter.6.cloned.1.call-update) | async-done | bytes 524304 | tf_op jit(solution)/shard_map/reduce_scatter | solution.py:48
  425.3 109.6 %reduce-scatter.8.cloned.1.call-done = bf16[128,2048]{1,0:T(8,128)(2,1)} async-done(((bf16[2048,2048]{1,0:T(8,128)(2,1)}), bf16[128,2048]{1,0:T(8,128)(2,1)}) %reduce-scatter.8.cloned.1.call-update) | async-done | bytes 524304 | tf_op jit(solution)/shard_map/reduce_scatter | solution.py:48
  (8 shorter events, 0.0 us)
Async XLA Ops:
  7.2 165.6 %copy-start = (bf16[1,704,2048]{2,1,0:T(8,128)(2,1)S(1)}, bf16[1,704,2048]{2,1,0:T(8,128)(2,1)}, u32[]{:S(2)}) copy-start(bf16[1,704,2048]{2,1,0:T(8,128)(2,1)} %param.13) | copy-start | bytes 8650756
  7.2 78.9 %all-gather.5.cloned.1.call-start = ((), (), s32[]{:S(2)}) async-start(), calls=%async_computation.9 | async-start | bytes 8912896 | tf_op jit(solution)/shard_map/all_gather | solution.py:28
  7.9 153.5 %all-gather.3.cloned.1.call-start = ((), (), s32[]{:S(2)}) async-start(), calls=%async_computation.7 | async-start | bytes 8912896 | tf_op jit(solution)/shard_map/all_gather | solution.py:27
  8.7 231.9 %reduce-scatter.14.cloned.1.call-start = ((), (), s32[]{:S(2)}) async-start(), calls=%async_computation.13 | async-start | bytes 4325376 | tf_op jit(solution)/shard_map/reduce_scatter | solution.py:56
  161.4 4.8 copy-start.10
  166.2 3.2 copy-start.1
  166.2 3.3 copy-start.9
  169.6 3.2 copy-start.4
  169.6 3.2 copy-start.2
  172.7 5.2 copy-start.5
  178.5 7.0 %copy-start.3 = (bf16[16,64,2048]{2,1,0:T(8,128)(2,1)S(1)}, bf16[16,64,2048]{2,1,0:T(8,128)(2,1)}, u32[]{:S(2)}) copy-start(bf16[16,64,2048]{2,1,0:T(8,128)(2,1)} %convolution_convert_fusion.3) | copy-start | bytes 12582916
  184.4 1.1 copy-start.7
  190.0 82.3 %reduce-scatter.12.cloned.1.call-start = ((), (), s32[]{:S(2)}) async-start(), calls=%async_computation.12 | async-start | bytes 4325376 | tf_op jit(solution)/shard_map/reduce_scatter | solution.py:56
  197.4 118.1 %reduce-scatter.10.cloned.1.call-start = ((), (), s32[]{:S(2)}) async-start(), calls=%async_computation.11 | async-start | bytes 4325376 | tf_op jit(solution)/shard_map/reduce_scatter | solution.py:56
  204.8 220.5 %reduce-scatter.6.cloned.1.call-start = ((), (), s32[]{:S(2)}) async-start(), calls=%async_computation.8 | async-start | bytes 8912896 | tf_op jit(solution)/shard_map/reduce_scatter | solution.py:48
  215.7 319.3 %reduce-scatter.8.cloned.1.call-start = ((), (), s32[]{:S(2)}) async-start(), calls=%async_computation.10 | async-start | bytes 8912896 | tf_op jit(solution)/shard_map/reduce_scatter | solution.py:48
  215.9 5.9 %copy-start.6 = (bf16[1024,704]{0,1:T(8,128)(2,1)S(1)}, bf16[1024,704]{0,1:T(8,128)(2,1)}, u32[]{:S(2)}) copy-start(bf16[1024,704]{0,1:T(8,128)(2,1)} %get-tuple-element.10) | copy-start | bytes 4325380
  215.9 5.9 %copy-start.11 = (bf16[1,2048,704]{1,2,0:T(8,128)(2,1)S(1)}, bf16[1,2048,704]{1,2,0:T(8,128)(2,1)}, u32[]{:S(2)}) copy-start(bf16[1,2048,704]{1,2,0:T(8,128)(2,1)} %param.12) | copy-start | bytes 8650756
  231.2 8.7 %copy-start.8 = (s32[128,6]{0,1:T(8,128)S(1)}, s32[128,6]{0,1:T(8,128)}, u32[]{:S(2)}) copy-start(s32[128,6]{0,1:T(8,128)} %param.8) | copy-start | bytes 9220
Sparse Core Ops, SparseCore 0:
  10.2 75.8 all-gather.4
  88.2 73.1 all-gather.2
  190.1 38.8 reduce-scatter.13
  231.8 40.4 reduce-scatter.11
  274.9 40.4 reduce-scatter.9
  320.5 104.7 reduce-scatter.5
  430.5 104.4 reduce-scatter.7
